TPU v7x, 32 devices: a whole 2x2x4 slice. The times are simulated.
32 devices in a mesh: band: 4 (over y, x), pw: 8 (over z, core).
Axes of the slice: x: 2, y: 2, z: 4, core: 2. Of those that a mesh axis runs over, the one named last changes fastest.
Arguments:
- psi: float32 [2, 8, 16384], P(None, None, 'pw'), may hold values from -60 to 60
- energies: float32 [8], P('band'), may hold values from -2 to 0
- kinetic: float32 [16384], P('pw'), may hold values from 0.05 to 20
- vloc: float32 [128, 128, 128], P('pw'), may hold values from 0.5 to 2
- dv: float32 [128, 128, 128], P('pw'), may hold values from -5 to 5
- beta: float32 [2, 64, 16384], P(None, None, 'pw'), may hold values from -0.046875 to 0.046875
- nl_diag: float32 [64], replicated, may hold values from 1 to 10
- nl_coupling: float32 [64], replicated, may hold values from -4 to 4
- proj_counts: int32 [16], replicated, may hold values from 1 to 13, 64 in all
- pw_map: int32 [16384], P('pw'), may hold values from 0 to 16383, as said below
- stick_pos: int32 [1024], replicated, may hold values from 0 to 16383, as said below
Outputs:
- dpsi: float32 [2, 8, 16384], P(None, 'band', 'pw')
- residual: float32 [2, 8, 16384], P(None, 'band', 'pw')
- drho: float32 [128, 128, 128], P('pw', 'band')
Inputs may be any that keep to these rules, and one draw needn't show every extreme that they name: `pw_map`: within each block of 2048 entries (the plane waves of one pw index) the values are distinct, and each block holds 0 and 16383. `stick_pos`: all values distinct; 0 and 16383 appear.
All inputs are finite; a program needn't handle non-finite values.
Results may differ from a plain program's by a relative error of at most 0.0003.
Values sent between devices are 32-bit elements; how exact they have to be, the bound alone decides.
A program may use at most 256 MiB of HBM per device.

v0:
```python
import math

import jax
import jax.numpy as jnp
from jax import lax
from jax.sharding import PartitionSpec as P

ITERS = 2


PRECISE = lax.Precision.HIGHEST
ALPHA_SHIFT = 4.0


def dft_tables(length):
    positions = jnp.arange(length, dtype=jnp.int32)
    phases = positions[:, None] * positions[None, :] % length
    angles = phases.astype(jnp.float32) * (2.0 * math.pi / length)
    return (jnp.cos(angles), jnp.sin(angles))


def complex_transform(values_in, tables, direction_sign, einsum_form):
    cosine_table, sine_table = tables
    real_part, imag_part = (values_in[0], values_in[1])

    def product(table, operand):
        return jnp.einsum(einsum_form, table, operand, precision=PRECISE)

    return jnp.stack(
        [
            product(cosine_table, real_part) - direction_sign * product(sine_table, imag_part),
            product(cosine_table, imag_part) + direction_sign * product(sine_table, real_part),
        ]
    )


def project_onto(basis, vector):

    def product(left, right):
        return jnp.einsum("kg,ng->kn", left, right, precision=PRECISE)

    return jnp.stack(
        [
            product(basis[0], vector[0]) + product(basis[1], vector[1]),
            product(basis[0], vector[1]) - product(basis[1], vector[0]),
        ]
    )


def expand(basis, weights):

    def product(left, right):
        return jnp.einsum("kn,kg->ng", left, right, precision=PRECISE)

    return jnp.stack(
        [
            product(weights[0], basis[0]) - product(weights[1], basis[1]),
            product(weights[0], basis[1]) + product(weights[1], basis[0]),
        ]
    )


def dot_bands(left, right):
    return jnp.sum(left * right, axis=(0, 2))


def shards(
    psi, energies, kinetic, vloc, dv, beta, nl_diag, nl_coupling, proj_counts, pw_map, stick_pos
):
    grid_size = vloc.shape[1]
    plane_count = vloc.shape[0]
    columns = stick_pos.shape[0] // lax.axis_size("pw")
    total_pw = kinetic.shape[0] * lax.axis_size("pw")
    block_bands = energies.shape[0]
    norm_scale = 1.0 / math.sqrt(grid_size**3)
    tables = dft_tables(grid_size)
    own_states = lax.dynamic_slice_in_dim(psi, lax.axis_index("band") * block_bands, block_bands, 1)
    block_ends = jnp.cumsum(proj_counts)
    proj_index = jnp.arange(beta.shape[1], dtype=jnp.int32)
    atom_of = jnp.sum((proj_index[:, None] >= block_ends[None, :]).astype(jnp.int32), axis=1)
    same_atom = (atom_of[:, None] == atom_of[None, :]).astype(jnp.float32)

    def to_sticks(coeffs):
        item_count = coeffs.shape[1]
        flat_grid = (
            jnp.zeros((2, item_count, grid_size * columns), jnp.float32)
            .at[:, :, pw_map]
            .set(coeffs)
        )
        sticks = flat_grid.reshape(2, item_count, grid_size, columns)
        return complex_transform(sticks, tables, 1.0, "zk,bks->bzs")

    def planes_inverse(received):
        item_count = received.shape[1]
        flat_grid = jnp.zeros((2, item_count, plane_count, grid_size * grid_size), jnp.float32)
        flat_grid = flat_grid.at[:, :, :, stick_pos].set(received)
        field = flat_grid.reshape(2, item_count, plane_count, grid_size, grid_size)
        field = complex_transform(field, tables, 1.0, "yk,bpkx->bpyx")
        field = complex_transform(field, tables, 1.0, "xk,bpyk->bpyx")
        return field * norm_scale

    def planes_forward(field):
        item_count = field.shape[1]
        spectrum = complex_transform(field, tables, -1.0, "yk,bpkx->bpyx")
        spectrum = complex_transform(spectrum, tables, -1.0, "xk,bpyk->bpyx")
        spectrum = spectrum.reshape(2, item_count, plane_count, grid_size * grid_size)
        return jnp.take(spectrum, stick_pos, axis=3)

    def with_potential(potential):

        def apply_field(received):
            field = planes_inverse(received)
            return (field, planes_forward(field * potential))

        return apply_field

    def real_space(coeffs, plane_fn):
        return plane_fn(
            lax.all_to_all(to_sticks(coeffs), "pw", split_axis=2, concat_axis=3, tiled=True)
        )

    def from_sticks(back_values):
        sticks = lax.all_to_all(back_values, "pw", split_axis=3, concat_axis=2, tiled=True)
        item_count = sticks.shape[1]
        spectrum = complex_transform(sticks, tables, -1.0, "zk,bks->bzs") * norm_scale
        spectrum = spectrum.reshape(2, item_count, grid_size * columns)
        return jnp.take(spectrum, pw_map, axis=2)

    def projections(vector):
        return lax.psum((project_onto(psi, vector), project_onto(beta, vector)), "pw")

    def preconditioned_norm(residual, precond_res):
        return lax.psum(dot_bands(residual, precond_res), "pw")

    diagonal_shift = kinetic[None, None, :] - energies[None, :, None]
    precond = 1.0 / (1.0 + diagonal_shift)
    state_planes, dv_back = real_space(own_states, with_potential(dv))
    dvpsi = from_sticks(dv_back)
    rhs_state, rhs_beta = projections(dvpsi)
    rhs = -(dvpsi - expand(psi, rhs_state) / total_pw)
    solution = jnp.zeros_like(rhs)
    residual = rhs
    search = precond * residual
    norm_now = preconditioned_norm(residual, search)
    for iteration in range(ITERS):
        search_planes, local_back = real_space(search, with_potential(vloc))
        local_part = from_sticks(local_back)
        state_proj, beta_proj = projections(search)
        weighted = nl_coupling[None, :, None] * beta_proj
        grouped = jnp.einsum("ij,cjn->cin", same_atom, weighted, precision=PRECISE)
        nonlocal_part = expand(
            beta, nl_diag[None, :, None] * beta_proj + nl_coupling[None, :, None] * grouped
        )
        occupied_part = ALPHA_SHIFT / total_pw * expand(psi, state_proj)
        image = diagonal_shift * search + local_part + nonlocal_part + occupied_part
        step_len = norm_now / lax.psum(dot_bands(search, image), "pw")
        solution = solution + step_len[None, :, None] * search
        residual = residual - step_len[None, :, None] * image
        if iteration + 1 < ITERS:
            precond_res = precond * residual
            norm_next = preconditioned_norm(residual, precond_res)
            ratio = norm_next / norm_now
            search = precond_res + ratio[None, :, None] * search
            norm_now = norm_next
    solution_planes = real_space(solution, planes_inverse)
    density_scale = 2.0 * grid_size**3 / total_pw
    density_term = density_scale * jnp.sum(state_planes * solution_planes, axis=(0, 1))
    drho = lax.psum_scatter(density_term, "band", scatter_dimension=1, tiled=True)
    return (solution, residual, drho)


def solution(mesh):
    placed = (
        P(None, None, "pw"),
        P("band"),
        P("pw"),
        P("pw", None, None),
        P("pw", None, None),
        P(None, None, "pw"),
        P(),
        P(),
        P(),
        P("pw"),
        P(),
    )
    return jax.shard_map(
        shards,
        mesh=mesh,
        in_specs=placed,
        out_specs=(P(None, "band", "pw"), P(None, "band", "pw"), P("pw", "band", None)),
        check_vma=False,
    )
```

profile of v0, /device:TPU:0, one launch (start us, length us, event | category | flops | bytes accessed | tf_op | source)
XLA Modules:
  0.0 2318.5 jit_solution(12426958503764950152)
XLA Ops:
  15.2 186.6 %scatter_fusion = f32[2,2,16384]{1,0,2:T(2,128)} fusion(f32[2,2,16384]{1,0,2:T(2,128)} %broadcast.134.clone, s32[2048]{0:T(1024)S(1)} %get-tuple-element.45, f32[2048,2,2]{2,1,0:T(2,128)S(1)} %copy.624), kind=kCustom, calls=%fused_computation.6 | custom fusion | bytes 106496 | tf_op jit(solution)/shard_map/scatter | solution.py:88
  201.9 19.3 fusion.792
  252.5 11.0 broadcast.131.clone
  263.5 93.7 %scatter_fusion.1 = f32[2,2,16,16384]{2,1,3,0:T(2,128)} fusion(f32[2,2,16,16384]{2,1,3,0:T(2,128)} %broadcast.131.clone, s32[1024]{0:T(1024)S(1)} %get-tuple-element.47, f32[1024,2,2,16]{3,2,1,0:T(2,128)S(1)} %copy.634), kind=kCustom, calls=%fused_computation.7 | custom fusion | bytes 790528 | tf_op jit(solution)/shard_map/scatter | solution.py:96
  357.2 23.1 fusion.788
  380.3 13.2 copy.767
  398.3 13.4 copy.769
  483.2 36.1 %copy.653 = f32[2,2,16,16384]{2,1,3,0:T(2,128)} copy(f32[2,2,16,16384]{3,2,1,0:T(8,128)} %pad_maximum_fusion.1) | data formatting | bytes 8388608 | tf_op jit(solution)/shard_map/stack | solution.py:29
  519.3 17.8 gather_fusion
  568.0 14.9 copy.661
  582.8 12.7 gather_fusion.1
  597.5 14.7 psum.63
  621.8 186.6 %scatter_fusion.2 = f32[2,2,16384]{1,0,2:T(2,128)} fusion(f32[2,2,16384]{1,0,2:T(2,128)} %broadcast.134.clone.1, s32[2048]{0:T(1024)S(1)} %get-tuple-element.45, f32[2048,2,2]{2,1,0:T(2,128)S(1)} %copy.663), kind=kCustom, calls=%fused_computation.8 | custom fusion | bytes 106496 | tf_op jit(solution)/shard_map/scatter | solution.py:88
  808.4 19.3 fusion.791
  846.3 17.4 all-reduce.2
  868.6 11.0 broadcast.131.clone.1
  879.6 93.7 %scatter_fusion.3 = f32[2,2,16,16384]{2,1,3,0:T(2,128)} fusion(f32[2,2,16,16384]{2,1,3,0:T(2,128)} %broadcast.131.clone.1, s32[1024]{0:T(1024)S(1)} %get-tuple-element.47, f32[1024,2,2,16]{3,2,1,0:T(2,128)S(1)} %copy.673), kind=kCustom, calls=%fused_computation.9 | custom fusion | bytes 790528 | tf_op jit(solution)/shard_map/scatter | solution.py:96
  973.3 23.1 fusion.787
  996.4 13.2 copy.793
  1014.6 13.6 copy.794
  1098.7 36.1 %copy.692 = f32[2,2,16,16384]{2,1,3,0:T(2,128)} copy(f32[2,2,16,16384]{3,2,1,0:T(8,128)} %pad_maximum_fusion.2) | data formatting | bytes 8388608 | tf_op jit(solution)/shard_map/stack | solution.py:29
  1134.9 17.8 gather_fusion.2
  1186.6 14.9 copy.700
  1201.5 12.6 gather_fusion.3
  1215.2 14.5 all-reduce.1
  1230.0 13.9 psum.68
  1252.6 186.6 %scatter_fusion.4 = f32[2,2,16384]{1,0,2:T(2,128)} fusion(f32[2,2,16384]{1,0,2:T(2,128)} %broadcast.134.clone.2, s32[2048]{0:T(1024)S(1)} %get-tuple-element.45, f32[2048,2,2]{2,1,0:T(2,128)S(1)} %copy.703), kind=kCustom, calls=%fused_computation.10 | custom fusion | bytes 106496 | tf_op jit(solution)/shard_map/scatter | solution.py:88
  1439.2 19.3 fusion.790
  1477.1 17.5 all-reduce
  1499.6 11.0 broadcast.131.clone.2
  1510.6 93.7 %scatter_fusion.5 = f32[2,2,16,16384]{2,1,3,0:T(2,128)} fusion(f32[2,2,16,16384]{2,1,3,0:T(2,128)} %broadcast.131.clone.2, s32[1024]{0:T(1024)S(1)} %get-tuple-element.47, f32[1024,2,2,16]{3,2,1,0:T(2,128)S(1)} %copy.713), kind=kCustom, calls=%fused_computation.11 | custom fusion | bytes 790528 | tf_op jit(solution)/shard_map/scatter | solution.py:96
  1604.3 23.1 fusion.786
  1627.4 13.2 copy.817
  1645.5 13.4 copy.818
  1729.7 36.1 %copy.732 = f32[2,2,16,16384]{2,1,3,0:T(2,128)} copy(f32[2,2,16,16384]{3,2,1,0:T(8,128)} %pad_maximum_fusion.3) | data formatting | bytes 8388608 | tf_op jit(solution)/shard_map/stack | solution.py:29
  1765.8 17.8 gather_fusion.4
  1813.8 14.9 copy.740
  1828.7 12.6 gather_fusion.5
  1842.3 14.5 psum.71
  1864.7 186.6 %scatter_fusion.6 = f32[2,2,16384]{1,0,2:T(2,128)} fusion(f32[2,2,16384]{1,0,2:T(2,128)} %broadcast.134, s32[2048]{0:T(1024)S(1)} %get-tuple-element.45, f32[2048,2,2]{2,1,0:T(2,128)S(1)} %copy.742), kind=kCustom, calls=%fused_computation.12 | custom fusion | bytes 106496 | tf_op jit(solution)/shard_map/scatter | solution.py:88
  2051.3 19.3 fusion.789
  2083.5 12.1 all_to_all.117
  2097.0 11.0 broadcast.131
  2108.0 93.7 %scatter_fusion.7 = f32[2,2,16,16384]{2,1,3,0:T(2,128)} fusion(f32[2,2,16,16384]{2,1,3,0:T(2,128)} %broadcast.131, s32[1024]{0:T(1024)S(1)} %get-tuple-element.47, f32[1024,2,2,16]{3,2,1,0:T(2,128)S(1)} %copy.752), kind=kCustom, calls=%fused_computation.13 | custom fusion | bytes 790528 | tf_op jit(solution)/shard_map/scatter | solution.py:96
  2201.7 23.1 fusion.785
  2224.9 13.2 copy.841
  2243.0 13.6 copy.842
  2284.6 26.8 %reduce-scatter.2.cloned.1.call-done = f32[16,32,128]{2,1,0:T(8,128)} async-done(((f32[16,128,128]{2,1,0:T(8,128)}), f32[16,32,128]{2,1,0:T(8,128)}) %reduce-scatter.2.cloned.1.call-update) | async-done | bytes 262160 | tf_op jit(solution)/shard_map/reduce_scatter | solution.py:168
  (320 shorter events, 485.4 us)
Async XLA Ops:
  7.2 2.1 copy-start.26
  232.1 9.2 copy-start.27
  232.2 9.2 copy-start.23
  233.3 8.2 copy-start.29
  233.3 8.4 copy-start.24
  234.7 16.3 all-to-all-start
  393.5 4.9 copy-start.2
  411.7 3.7 copy-start.3
  422.6 4.0 copy-start.16
  433.8 3.8 copy-start.10
  437.6 1.4 copy-start.12
  476.3 2.9 copy-start.20
  542.3 7.3 copy-start.28
  542.3 7.3 copy-start.30
  545.9 13.2 all-to-all-start.1
  582.8 13.6 copy-start.1
  582.8 30.7 %copy-start = (f32[2,64,2048]{2,1,0:T(8,128)S(1)}, f32[2,64,2048]{2,1,0:T(8,128)}, u32[]{:S(2)}) copy-start(f32[2,64,2048]{2,1,0:T(8,128)} %param.20) | copy-start | bytes 3145732
  838.7 24.9 %copy-start.31 = (f32[64]{0:T(128)S(1)}, f32[64]{0:T(128)}, u32[]{:S(2)}) copy-start(f32[64]{0:T(128)} %param.22) | copy-start | bytes 772
  838.7 24.9 %copy-start.32 = (f32[64]{0:T(128)S(1)}, f32[64]{0:T(128)}, u32[]{:S(2)}) copy-start(f32[64]{0:T(128)} %param.21) | copy-start | bytes 772
  841.2 23.9 %all-to-all-start.2 = ((f32[2,2,128,128]{3,1,0,2:T(2,128)}), f32[2,2,128,128]{3,1,0,2:T(2,128)S(1)}, u32[]{:S(2)}, u32[]{:S(2)}) async-start(f32[2,2,128,128]{3,1,0,2:T(2,128)} %copy.670), calls=%async_computation.2 | async-start | bytes 524288 | tf_op jit(solution)/shard_map/all_to_all | solution.py:119
  1009.6 4.9 copy-start.4
  1028.2 3.7 copy-start.5
  1039.0 3.8 copy-start.17
  1050.1 3.8 copy-start.14
  1091.9 2.9 copy-start.21
  1161.5 13.3 all-to-all-start.3
  1472.0 24.1 %all-to-all-start.4 = ((f32[2,2,128,128]{3,1,0,2:T(2,128)}), f32[2,2,128,128]{3,1,0,2:T(2,128)S(1)}, u32[]{:S(2)}, u32[]{:S(2)}) async-start(f32[2,2,128,128]{3,1,0,2:T(2,128)} %copy.710), calls=%async_computation.4 | async-start | bytes 524288 | tf_op jit(solution)/shard_map/all_to_all | solution.py:119
  1640.6 4.9 copy-start.6
  1658.9 3.7 copy-start.7
  1669.7 3.8 copy-start.18
  1680.8 4.0 copy-start.15
  1722.8 2.9 copy-start.22
  1792.4 13.1 all-to-all-start.5
  1795.8 515.6 %reduce-scatter.2.cloned.1.call-start = ((), (), s32[]{:S(2)}) async-start(), calls=%async_computation.8 | async-start | bytes 1310720 | tf_op jit(solution)/shard_map/reduce_scatter | solution.py:168
  1857.6 7.1 copy-start.25
  2238.0 4.9 copy-start.8
  2256.6 3.7 copy-start.9
  2267.4 3.8 copy-start.19
  2278.5 3.9 copy-start.11
  2278.5 3.9 copy-start.13
Sparse Core Ops, SparseCore 0:
  2284.7 26.6 reduce-scatter.1
where the time goes:
time: 2350 us; the launch traced here: 2320 us
  local copies, waits for them, and re-layouts  1820 us (77%)
  matrix products  254 us (11%)
  blocking collectives  105 us (4%)
  waiting for transfers between devices  61.7 us (3%)
  other arithmetic  39.9 us (2%)
  starting transfers between devices  24.3 us (1%)
    scatter x4, local copies, waits for them, and re-layouts, to_sticks(): flat_grid = jnp.zeros((2, item_count, grid_size * columns), jnp.float32)....  747 us
    scatter x4, local copies, waits for them, and re-layouts, planes_inverse(): flat_grid = flat_grid.at[:, :, :, stick_pos].set(received)  375 us
    dot_general x84, matrix products, product(): return jnp.einsum(einsum_form, table, operand, precision=PRECISE)  241 us
    slice x11, local copies, waits for them, and re-layouts, complex_transform(): real_part, imag_part = (values_in[0], values_in[1])  170 us
    squeeze x16, local copies, waits for them, and re-layouts, complex_transform(): real_part, imag_part = (values_in[0], values_in[1])  149 us
    another operation x19, local copies, waits for them, and re-layouts, complex_transform(): jnp.stack([product(cosine_table, real_part) - direction_sign * product(si...  128 us
    another operation x9, local copies, waits for them, and re-layouts  68.1 us
    gather x3, local copies, waits for them, and re-layouts, planes_forward(): return jnp.take(spectrum, stick_pos, axis=3)  53.4 us
  transfers between devices with their start and end apart: 7, of which 5 were waited for; matrix products, arithmetic and copies ran while one was open for 0% of the time, Pallas kernels for 0%

commit v1 on v0

v1 whole, which is shorter than its diff:
```python
import functools
import math

import jax
import jax.numpy as jnp
import numpy as np
from jax import lax
from jax.experimental import pallas as pl
from jax.experimental.pallas import tpu as pltpu
from jax.sharding import PartitionSpec as P

ITERS = 2
PRECISE = lax.Precision.HIGH
ALPHA_SHIFT = 4.0
UNROLL = 16
KY_BLOCK = 32


def split(value):
    high = value.astype(jnp.bfloat16)
    return high, (value - high.astype(jnp.float32)).astype(jnp.bfloat16)


def dot32(left, right):
    return jnp.dot(left, right, preferred_element_type=jnp.float32)


def data_table(value, table_ref):
    high, low = split(value)
    return dot32(high, table_ref[0]) + dot32(low, table_ref[0]) + dot32(high, table_ref[1])


def table_data(table_ref, value):
    high, low = split(value)
    return dot32(table_ref[0], high) + dot32(table_ref[0], low) + dot32(table_ref[1], high)


def block_tables(length, scale):
    positions = np.arange(length)
    angles = (positions[:, None] * positions[None, :] % length) * (2.0 * math.pi / length)
    cosine, sine = np.cos(angles) * scale, np.sin(angles) * scale
    inverse_right = np.block([[cosine, sine], [-sine, cosine]])
    forward_right = np.block([[cosine, -sine], [sine, cosine]])
    stacked = np.stack([inverse_right, forward_right, inverse_right.T, forward_right.T]).astype(np.float32)
    high = stacked.astype(jnp.bfloat16)
    low = (stacked - high.astype(np.float32)).astype(jnp.bfloat16)
    return jnp.asarray(np.stack([high, low], axis=1))


def plane_kernel(size, planes, bands, mode, pos_ref, rows_ref, pot_ref, table_ref, *rest):
    items = bands * planes
    if mode == "first":
        back_ref, field_ref, grid_ref, mid_ref = rest
    else:
        state_ref, back_ref, energy_ref, density_ref, grid_ref, mid_ref = rest
        energy_ref[...] = jnp.zeros_like(energy_ref)
    sticks = rows_ref.shape[0]
    zero_rows = 512

    def clear(step, carry):
        grid_ref[pl.ds(pl.multiple_of(step * zero_rows, zero_rows), zero_rows), :] = jnp.zeros(
            (zero_rows, 2 * items), jnp.float32
        )
        return carry

    lax.fori_loop(0, size * size // zero_rows, clear, 0)

    def put(step, carry):
        for offset in range(UNROLL):
            stick = step * UNROLL + offset
            grid_ref[pl.ds(pos_ref[stick], 1), :] = rows_ref[pl.ds(stick, 1), :]
        return carry

    lax.fori_loop(0, sticks // UNROLL, put, 0)

    def x_inverse(step, carry):
        parts = []
        for offset in range(KY_BLOCK):
            start = pl.multiple_of((step * KY_BLOCK + offset) * size, size)
            turned = grid_ref[pl.ds(start, size), :].T
            parts.append(jnp.concatenate([turned[:items], turned[items:]], axis=1))
        result = data_table(jnp.concatenate(parts, axis=0), table_ref.at[0])
        height = KY_BLOCK * items
        for half in range(2):
            mid_ref[half, pl.ds(pl.multiple_of(step * height, height), height), :] = result[
                :, half * size : (half + 1) * size
            ]
        return carry

    lax.fori_loop(0, size // KY_BLOCK, x_inverse, 0)

    def y_stage(plane, carry):
        loads = []
        for band in range(bands):
            where = pl.ds(band * planes + plane, size, stride=items)
            loads.append(jnp.concatenate([mid_ref[0, where, :], mid_ref[1, where, :]], axis=0))
        field = table_data(table_ref.at[2], jnp.concatenate(loads, axis=1))
        potential = pot_ref[plane]
        wide = jnp.concatenate([potential] * bands, axis=1)
        shaped = field * jnp.concatenate([wide, wide], axis=0)
        if mode == "first":
            field_ref[plane] = field
        else:
            product = field * state_ref[plane]
            total = product[:size] + product[size:]
            height = density_ref.shape[3]
            for band in range(bands):
                for slab in range(density_ref.shape[1]):
                    density_ref[band, slab, plane] = total[
                        slab * height : (slab + 1) * height, band * size : (band + 1) * size
                    ]
            energy = (field * shaped).reshape(2 * size // 8, 8, bands * size)
            energy_ref[...] += jnp.sum(energy, axis=0)
        spectrum = table_data(table_ref.at[3], shaped)
        for band in range(bands):
            where = pl.ds(band * planes + plane, size, stride=items)
            for half in range(2):
                mid_ref[half, where, :] = spectrum[
                    half * size : (half + 1) * size, band * size : (band + 1) * size
                ]
        return carry

    lax.fori_loop(0, planes, y_stage, 0, unroll=4)

    def x_forward(step, carry):
        height = KY_BLOCK * items
        where = pl.ds(pl.multiple_of(step * height, height), height)
        result = data_table(
            jnp.concatenate([mid_ref[0, where, :], mid_ref[1, where, :]], axis=1), table_ref.at[1]
        )
        for offset in range(KY_BLOCK):
            piece = result[offset * items : (offset + 1) * items]
            start = pl.multiple_of((step * KY_BLOCK + offset) * size, size)
            grid_ref[pl.ds(start, size), :] = jnp.concatenate(
                [piece[:, :size], piece[:, size:]], axis=0
            ).T
        return carry

    lax.fori_loop(0, size // KY_BLOCK, x_forward, 0)

    def take(step, carry):
        for offset in range(UNROLL):
            stick = step * UNROLL + offset
            back_ref[pl.ds(stick, 1), :] = grid_ref[pl.ds(pos_ref[stick], 1), :]
        return carry

    lax.fori_loop(0, sticks // UNROLL, take, 0)


def plane_call(mode, size, planes, bands, positions, rows, potential, tables, *state):
    items = bands * planes
    back = jax.ShapeDtypeStruct(rows.shape, jnp.float32)
    field = jax.ShapeDtypeStruct((planes, 2 * size, bands * size), jnp.float32)
    energy = jax.ShapeDtypeStruct((8, bands * size), jnp.float32)
    slabs = lax.axis_size("band")
    density = jax.ShapeDtypeStruct((bands, slabs, planes, size // slabs, size), jnp.float32)
    shapes = {"first": (back, field), "apply": (back, energy, density)}[mode]
    vmem = pl.BlockSpec(memory_space=pltpu.VMEM)
    return pl.pallas_call(
        functools.partial(plane_kernel, size, planes, bands, mode),
        out_shape=shapes,
        in_specs=[pl.BlockSpec(memory_space=pltpu.SMEM), vmem, vmem, vmem] + [vmem for _ in state],
        out_specs=tuple(vmem for _ in shapes),
        scratch_shapes=[
            pltpu.VMEM((size * size, 2 * items), jnp.float32),
            pltpu.VMEM((2, size * items, size), jnp.float32),
        ],
        compiler_params=pltpu.CompilerParams(vmem_limit_bytes=48 * 2**20),
        name="plane_" + mode,
    )(positions, rows, potential, tables, *state)


def project_onto(basis, vector):
    def product(left, right):
        return jnp.einsum("kg,ng->kn", left, right, precision=PRECISE)

    return jnp.stack(
        [
            product(basis[0], vector[0]) + product(basis[1], vector[1]),
            product(basis[0], vector[1]) - product(basis[1], vector[0]),
        ]
    )


def expand(basis, weights):
    def product(left, right):
        return jnp.einsum("kn,kg->ng", left, right, precision=PRECISE)

    return jnp.stack(
        [
            product(weights[0], basis[0]) - product(weights[1], basis[1]),
            product(weights[0], basis[1]) + product(weights[1], basis[0]),
        ]
    )


def dot_bands(left, right):
    return jnp.sum(left * right, axis=(0, 2))


def shards(
    psi, energies, kinetic, vloc, dv, beta, nl_diag, nl_coupling, proj_counts, pw_map, stick_pos
):
    size = vloc.shape[1]
    plane_count = vloc.shape[0]
    groups = lax.axis_size("pw")
    columns = stick_pos.shape[0] // groups
    total_pw = kinetic.shape[0] * groups
    bands = energies.shape[0]
    padded = plane_count
    while bands * padded % 8:
        padded += 1
    norm_scale = 1.0 / math.sqrt(size**3)
    tables = block_tables(size, 1.0)
    own_states = lax.dynamic_slice_in_dim(psi, lax.axis_index("band") * bands, bands, 1)
    atoms = jnp.arange(proj_counts.shape[0], dtype=jnp.int32)
    block_ends = jnp.sum(
        jnp.where(atoms[None, :] <= atoms[:, None], proj_counts[None, :], 0), axis=1
    )
    proj_index = jnp.arange(beta.shape[1], dtype=jnp.int32)
    atom_of = jnp.sum((proj_index[:, None] >= block_ends[None, :]).astype(jnp.int32), axis=1)
    same_atom = (atom_of[:, None] == atom_of[None, :]).astype(jnp.float32)

    grid_points = np.arange(size)
    angles = (grid_points[:, None] * grid_points[None, :] % size) * (2.0 * math.pi / size)
    both = norm_scale * np.concatenate([np.cos(angles), np.sin(angles)]).astype(np.float32)
    both_high = both.astype(jnp.bfloat16)
    both_low = (both - both_high.astype(np.float32)).astype(jnp.bfloat16)
    level = (
        jnp.arange(size, dtype=jnp.int32)[:, None] == (pw_map // columns)[None, :]
    ).astype(jnp.bfloat16)
    phases = jnp.dot(both_high, level, preferred_element_type=jnp.float32) + jnp.dot(
        both_low, level, preferred_element_type=jnp.float32
    )
    cos_zg, sin_zg = phases[:size], phases[size:]
    pick = (
        jnp.arange(columns, dtype=jnp.int32)[:, None] == (pw_map % columns)[None, :]
    ).astype(jnp.bfloat16)

    def halves(value):
        high = lax.reduce_precision(value, 8, 7)
        return high.astype(jnp.bfloat16), (value - high).astype(jnp.bfloat16)

    def selected(form, value, chooser):
        high, low = halves(value)
        return jnp.einsum(form, high, chooser, preferred_element_type=jnp.float32) + jnp.einsum(
            form, low, chooser, preferred_element_type=jnp.float32
        )

    def exchange(blocks, carried):
        lanes = blocks.shape[2]
        extra = -(-carried.shape[0] // lanes)
        extra += -extra % 8
        tail = jnp.pad(carried, (0, extra * lanes - carried.shape[0])).reshape(1, extra, lanes)
        tail = jnp.broadcast_to(tail, (groups, extra, lanes))
        moved = lax.all_to_all(
            jnp.concatenate([blocks, tail], axis=1), "pw", split_axis=0, concat_axis=0, tiled=True
        )
        total = jnp.sum(moved[:, columns:], axis=0).reshape(-1)
        return moved[:, :columns], total[: carried.shape[0]]

    def group_sum(value):
        flat = value.reshape(-1)
        height = -(-flat.shape[0] // 1024) * 8
        flat = jnp.pad(flat, (0, height * 128 - flat.shape[0])).reshape(1, height, 128)
        moved = lax.all_to_all(
            jnp.broadcast_to(flat, (groups, height, 128)), "pw", split_axis=0, concat_axis=0, tiled=True
        )
        return jnp.sum(moved, axis=0).reshape(-1)[: value.size].reshape(value.shape)

    def to_rows(coeffs, carried):
        real, imag = coeffs[0][:, None, :], coeffs[1][:, None, :]
        turned = jnp.stack(
            [real * cos_zg - imag * sin_zg, imag * cos_zg + real * sin_zg]
        )
        sticks = selected("cbzg,sg->cbzs", turned, pick)
        sticks = sticks.reshape(2, bands, groups, plane_count, columns)
        sticks = jnp.transpose(sticks, (2, 4, 0, 1, 3)).reshape(groups, columns, -1)
        if carried is None:
            rows = lax.all_to_all(sticks, "pw", split_axis=0, concat_axis=0, tiled=True)
            total = None
        else:
            rows, total = exchange(sticks, carried)
        rows = rows.reshape(groups * columns, 2, bands, plane_count)
        rows = jnp.pad(rows, ((0, 0), (0, 0), (0, 0), (0, padded - plane_count)))
        return rows.reshape(groups * columns, -1), total

    def from_rows(rows, carried):
        rows = rows.reshape(groups * columns, 2, bands, padded)[..., :plane_count]
        rows = rows.reshape(groups, columns, -1)
        if carried is None:
            sticks = lax.all_to_all(rows, "pw", split_axis=0, concat_axis=0, tiled=True)
            total = None
        else:
            sticks, total = exchange(rows, carried)
        sticks = sticks.reshape(groups, columns, 2, bands, plane_count)
        sticks = jnp.transpose(sticks, (2, 3, 0, 4, 1)).reshape(2, bands, size, columns)
        chosen = selected("cbzs,sg->cbzg", sticks, pick)
        coeffs = jnp.stack(
            [
                jnp.sum(chosen[0] * cos_zg + chosen[1] * sin_zg, axis=1),
                jnp.sum(chosen[1] * cos_zg - chosen[0] * sin_zg, axis=1),
            ]
        )
        return coeffs, total

    def pad_planes(value):
        return jnp.pad(value, ((0, padded - plane_count), (0, 0), (0, 0)))

    def couple(beta_proj):
        weighted = nl_coupling[None, :, None] * beta_proj
        grouped = jnp.einsum("ij,cjn->cin", same_atom, weighted, precision=PRECISE)
        return nl_diag[None, :, None] * beta_proj + nl_coupling[None, :, None] * grouped

    def send_vector(vector, residual):
        parts = (project_onto(psi, vector), project_onto(beta, vector), dot_bands(residual, vector))
        rows, total = to_rows(vector, jnp.concatenate([part.reshape(-1) for part in parts]))
        first = parts[0].size
        second = first + parts[1].size
        return (
            rows,
            total[:first].reshape(parts[0].shape),
            total[first:second].reshape(parts[1].shape),
            total[second:],
        )

    def weigh(steps, density):
        return sum(steps[band] * density[band, :, :plane_count] for band in range(bands))

    diagonal_shift = kinetic[None, None, :] - energies[None, :, None]
    precond = 1.0 / (1.0 + diagonal_shift)
    state_rows, _ = to_rows(own_states, None)
    back, state_planes = plane_call(
        "first", size, padded, bands, stick_pos, state_rows, pad_planes(dv), tables
    )
    dvpsi, _ = from_rows(back, None)
    rhs_state = group_sum(project_onto(psi, dvpsi))
    rhs = -(dvpsi - expand(psi, rhs_state) / total_pw)
    solution = jnp.zeros_like(rhs)
    residual = rhs
    search = precond * residual
    rows, state_proj, beta_proj, norm_now = send_vector(search, residual)
    local_potential = pad_planes(vloc)
    density_scale = 2.0 * size**3 / total_pw
    weighed = []
    for iteration in range(ITERS):
        local_back, energy, density = plane_call(
            "apply", size, padded, bands, stick_pos, rows, local_potential, tables, state_planes
        )
        coupled = couple(beta_proj)
        nonlocal_part = expand(beta, coupled)
        occupied_part = ALPHA_SHIFT / total_pw * expand(psi, state_proj)
        known_part = diagonal_shift * search + nonlocal_part + occupied_part
        own_energy = jnp.sum(energy.reshape(8, bands, size), axis=(0, 2))
        own_energy = own_energy + dot_bands(search, diagonal_shift * search)
        local_part, curvature = from_rows(local_back, own_energy)
        curvature = curvature + jnp.sum(beta_proj * coupled, axis=(0, 1))
        curvature = curvature + ALPHA_SHIFT / total_pw * jnp.sum(state_proj * state_proj, axis=(0, 1))
        image = known_part + local_part
        step_len = norm_now / curvature
        solution = solution + step_len[None, :, None] * search
        residual = residual - step_len[None, :, None] * image
        weighed.append((density_scale * step_len, density))
        if iteration + 1 < ITERS:
            precond_res = precond * residual
            new_rows, new_state, new_beta, norm_next = send_vector(precond_res, residual)
            ratio = norm_next / norm_now
            lanes = jnp.broadcast_to(ratio[None, :, None], (2, bands, padded)).reshape(-1)
            rows = new_rows + lanes[None, :] * rows
            state_proj = new_state + ratio * state_proj
            beta_proj = new_beta + ratio * beta_proj
            search = precond_res + ratio[None, :, None] * search
            norm_now = norm_next
    density_term = sum(weigh(steps, density) for steps, density in weighed)
    drho = jnp.sum(
        lax.all_to_all(density_term, "band", split_axis=0, concat_axis=0, tiled=True), axis=0
    )
    return (solution, residual, drho)


def solution(mesh):
    placed = (
        P(None, None, "pw"),
        P("band"),
        P("pw"),
        P("pw", None, None),
        P("pw", None, None),
        P(None, None, "pw"),
        P(),
        P(),
        P(),
        P("pw"),
        P(),
    )
    return jax.shard_map(
        shards,
        mesh=mesh,
        in_specs=placed,
        out_specs=(P(None, "band", "pw"), P(None, "band", "pw"), P("pw", "band", None)),
        check_vma=False,
    )
```

time: 2350 us -> 254 us (0.11); the launches traced: 2320 us -> 252 us
  local copies, waits for them, and re-layouts: 1820 us -> 18 us
  matrix products: 254 us -> 33 us
  blocking collectives: 105 us -> 28.2 us
  Pallas kernels: 0 us -> 62.4 us
    scatter x8 -> x0, local copies, waits for them, and re-layouts: 1120 us -> none  [the longest x4 747 us: to_sticks(): flat_grid = jnp.zeros((2, item_count, grid_size * columns), jnp.float32)....]
    dot_general x86 -> x16, matrix products: 242 us -> 12 us  [the longest x6 4.45 us: selected(): jnp.einsum(form, low, chooser, preferred_element_type=jnp.float32)]
    another operation x28 -> x8, local copies, waits for them, and re-layouts: 197 us -> 1.01 us  [the longest x3 0.53 us: from_rows(): rows = rows.reshape(groups, columns, -1)]
    slice x11 -> x17, local copies, waits for them, and re-layouts: 170 us -> 5.65 us  [the longest x6 1.43 us: exchange(): return (moved[:, :columns], total[:carried.shape[0]])]
    squeeze x16 -> x0, local copies, waits for them, and re-layouts: 149 us -> none  [complex_transform(): real_part, imag_part = (values_in[0], values_in[1])]
    gather x9 -> x0, local copies, waits for them, and re-layouts: 93.9 us -> none  [the longest x3 53.4 us: planes_forward(): return jnp.take(spectrum, stick_pos, axis=3)]
    psum x6 -> x0, blocking collectives: 92.5 us -> none  [the longest x3 49.6 us: projections(): lax.psum((project_onto(psi, vector), project_onto(beta, vector)), 'pw')]
    pallas_call x0 -> x3, Pallas kernels: none -> 62.4 us  [plane_call(): pl.pallas_call(functools.partial(plane_kernel, size, planes, bands, mode)...]
  transfers between devices with their start and end apart: 7 -> 6, of which waited for: 5 -> 6; matrix products, arithmetic and copies ran while one was open for 0% -> 6% of each run, Pallas kernels for 0% -> 0%
where the time goes in v1:
time: 254 us; the launch traced here: 252 us
  waiting for transfers between devices  63 us (25%)
  Pallas kernels  62.4 us (25%)
  matrix products  33 us (13%)
  blocking collectives  28.2 us (11%)
  other arithmetic  23 us (9%)
  starting transfers between devices  22.6 us (9%)
  local copies, waits for them, and re-layouts  18 us (7%)
    pallas_call x3, Pallas kernels, plane_call(): pl.pallas_call(functools.partial(plane_kernel, size, planes, bands, mode)...  62.4 us
    all_to_all x4, waiting for transfers between devices, exchange(): lax.all_to_all(jnp.concatenate([blocks, tail], axis=1), 'pw', split_axis=...  49.1 us
    all_to_all x1, blocking collectives, to_rows(): rows = lax.all_to_all(sticks, 'pw', split_axis=0, concat_axis=0, tiled=True)  16 us
    all_to_all x4, starting transfers between devices, exchange(): lax.all_to_all(jnp.concatenate([blocks, tail], axis=1), 'pw', split_axis=...  15.4 us
    dot_general x20, matrix products, product(): return jnp.einsum('kn,kg->ng', left, right, precision=PRECISE)  14.3 us
    all_to_all x1, blocking collectives, from_rows(): sticks = lax.all_to_all(rows, 'pw', split_axis=0, concat_axis=0, tiled=True)  12.1 us
    all_to_all x1, waiting for transfers between devices, shards(): lax.all_to_all(density_term, 'band', split_axis=0, concat_axis=0, tiled=T...  8.52 us
    dot_general x20, matrix products, product(): return jnp.einsum('kg,ng->kn', left, right, precision=PRECISE)  6.61 us
  transfers between devices with their start and end apart: 6, of which 6 were waited for; matrix products, arithmetic and copies ran while one was open for 6% of the time, Pallas kernels for 0%

profile of v1, /device:TPU:0, one launch (start us, length us, event | category | flops | bytes accessed | tf_op | source)
XLA Modules:
  0.0 252.1 jit_solution(750168035287421776)
XLA Ops:
  1.4 1.3 fusion.64
  6.6 16.0 %all_to_all.40 = f32[8,128,64]{1,2,0:T(8,128)S(1)} all-to-all(f32[8,128,64]{1,2,0:T(8,128)S(1)} %bitcast.344), channel_id=1, replica_groups=mesh['band'=4,'pw'=8] {'pw'}, dimensions={0} | all-to-all | bytes 524288 | tf_op jit(solution)/shard_map/all_to_all | solution.py:280
  22.8 21.0 %plane_first.1 = (f32[1024,64]{1,0:T(8,128)S(1)}, f32[16,256,256]{2,1,0:T(8,128)}) custom-call(s32[1024]{0:T(1024)S(1)} %copy-done.6, f32[1024,64]{1,0:T(8,128)S(1)} %bitcast.340, f32[16,128,128]{2,1,0:T(8,128)S(1)} %copy-done.5, bf16[4,2,256,256]{3,2,1,0:T(8,128)(2,1)S(1)} %copy-done), custom_call_target="tpu_custom_call" | custom-call | tf_op jit(solution)/shard_map/plane_first/pallas_call | solution.py:159
  44.0 12.1 %all_to_all.41 = f32[8,128,64]{1,2,0:T(8,128)S(1)} all-to-all(f32[8,128,64]{1,2,0:T(8,128)S(1)} %copy.168), channel_id=1, replica_groups=mesh['band'=4,'pw'=8] {'pw'}, dimensions={0} | all-to-all | bytes 524288 | tf_op jit(solution)/shard_map/all_to_all | solution.py:292
  60.9 3.5 %all-to-all-start.2 = ((f32[8,8,128]{2,1,0:T(8,128)}), f32[8,8,128]{2,1,0:T(8,128)S(1)}, u32[]{:S(2)}, u32[]{:S(2)}) async-start(f32[8,8,128]{2,1,0:T(8,128)} %broadcast_in_dim.35), calls=%async_computation.2 | async-start | bytes 65536 | tf_op jit(solution)/shard_map/all_to_all | solution.py:266
  64.5 5.4 %all-to-all-done.2 = f32[8,8,128]{2,1,0:T(8,128)S(1)} async-done(((f32[8,8,128]{2,1,0:T(8,128)}), f32[8,8,128]{2,1,0:T(8,128)S(1)}, u32[]{:S(2)}, u32[]{:S(2)}) %all-to-all-start.2) | async-done | bytes 32800 | tf_op jit(solution)/shard_map/all_to_all | solution.py:266
  69.9 0.9 slice.263
  70.8 1.0 fusion.153
  71.8 0.9 fusion.133
  72.7 0.9 fusion.13
  73.6 0.9 fusion.12
  79.8 0.8 pad_maximum_fusion.3
  80.6 3.5 %all-to-all-start.3 = ((f32[8,136,64]{1,2,0:T(8,128)}), f32[8,136,64]{1,2,0:T(8,128)S(1)}, u32[]{:S(2)}, u32[]{:S(2)}) async-start(f32[8,136,64]{1,2,0:T(8,128)} %pad_maximum_fusion.3), calls=%async_computation.3 | async-start | bytes 1048576 | tf_op jit(solution)/shard_map/all_to_all | solution.py:256
  84.9 14.5 %all-to-all-done.3 = f32[8,136,64]{1,2,0:T(8,128)S(1)} async-done(((f32[8,136,64]{1,2,0:T(8,128)}), f32[8,136,64]{1,2,0:T(8,128)S(1)}, u32[]{:S(2)}, u32[]{:S(2)}) %all-to-all-start.3) | async-done | bytes 278560 | tf_op jit(solution)/shard_map/all_to_all | solution.py:256
  100.5 0.8 fusion.146
  101.3 0.8 fusion.128
  102.4 20.7 %plane_apply.2 = (f32[1024,64]{1,0:T(8,128)S(1)}, f32[8,256]{1,0:T(8,128)S(1)}, f32[2,4,16,32,128]{4,3,2,1,0:T(8,128)S(1)}) custom-call(s32[1024]{0:T(1024)S(1)} %copy-done.6, f32[1024,64]{1,0:T(8,128)S(1)} %bitcast.339, f32[16,128,128]{2,1,0:T(8,128)S(1)} %copy-done.1, bf16[4,2,256,256]{3,2,1,0:T(8,128)(2,1)S(1)} %copy-done, ...), custom_call_target="tpu_custom_call" | custom-call | tf_op jit(solution)/shard_map/plane_apply/pallas_call | solution.py:159
  123.1 1.3 copy-done.2
  126.3 0.9 pad_maximum_fusion.4
  127.2 3.8 %all-to-all-start.4 = ((f32[8,136,64]{1,2,0:T(8,128)}), f32[8,136,64]{1,2,0:T(8,128)S(1)}, u32[]{:S(2)}, u32[]{:S(2)}) async-start(f32[8,136,64]{1,2,0:T(8,128)} %pad_maximum_fusion.4), calls=%async_computation.4 | async-start | bytes 1048576 | tf_op jit(solution)/shard_map/all_to_all | solution.py:256
  131.4 1.1 multiply_reduce_fusion.5
  132.5 1.3 fusion.84
  133.8 1.3 fusion.11
  135.1 0.9 fusion.9
  136.8 0.9 fusion.8
  137.7 1.3 fusion.71
  139.2 6.9 %all-to-all-done.4 = f32[8,136,64]{1,2,0:T(8,128)S(1)} async-done(((f32[8,136,64]{1,2,0:T(8,128)}), f32[8,136,64]{1,2,0:T(8,128)S(1)}, u32[]{:S(2)}, u32[]{:S(2)}) %all-to-all-start.4) | async-done | bytes 278560 | tf_op jit(solution)/shard_map/all_to_all | solution.py:256
  148.7 0.8 add_reduce_fusion.1
  153.6 1.4 fusion.43
  154.9 1.4 fusion.42
  157.0 0.9 pad_maximum_fusion.5
  157.9 3.5 %all-to-all-start.5 = ((f32[8,136,64]{1,2,0:T(8,128)}), f32[8,136,64]{1,2,0:T(8,128)S(1)}, u32[]{:S(2)}, u32[]{:S(2)}) async-start(f32[8,136,64]{1,2,0:T(8,128)} %pad_maximum_fusion.5), calls=%async_computation.5 | async-start | bytes 1048576 | tf_op jit(solution)/shard_map/all_to_all | solution.py:256
  162.0 14.6 %all-to-all-done.5 = f32[8,136,64]{1,2,0:T(8,128)S(1)} async-done(((f32[8,136,64]{1,2,0:T(8,128)}), f32[8,136,64]{1,2,0:T(8,128)S(1)}, u32[]{:S(2)}, u32[]{:S(2)}) %all-to-all-start.5) | async-done | bytes 278560 | tf_op jit(solution)/shard_map/all_to_all | solution.py:256
  177.4 1.4 fusion.164
  178.8 1.2 multiply_reduce_fusion.2
  180.1 0.8 fusion.139
  180.9 0.8 fusion.123
  182.8 20.7 %plane_apply.3 = (f32[1024,64]{1,0:T(8,128)S(1)}, f32[8,256]{1,0:T(8,128)S(1)}, f32[2,4,16,32,128]{4,3,2,1,0:T(8,128)S(1)}) custom-call(s32[1024]{0:T(1024)S(1)} %copy-done.6, f32[1024,64]{1,0:T(8,128)S(1)} %bitcast_add_fusion.rows_ref, f32[16,128,128]{2,1,0:T(8,128)S(1)} %copy-done.1, bf16[4,2,256,256]{3,2,1,0:T(8,128)(2,1)S(1)} %copy-done, ...), custom_call_target="tpu_custom_call" | custom-call | tf_op jit(solution)/shard_map/plane_apply/pallas_call | solution.py:159
  203.5 1.3 copy-done.4
  205.4 0.8 pad_maximum_fusion.6
  206.2 4.5 %all-to-all-start.6 = ((f32[8,136,64]{1,2,0:T(8,128)}), f32[8,136,64]{1,2,0:T(8,128)}, u32[]{:S(2)}, u32[]{:S(2)}) async-start(f32[8,136,64]{1,2,0:T(8,128)} %pad_maximum_fusion.6), calls=%async_computation.6 | async-start | bytes 1048576 | tf_op jit(solution)/shard_map/all_to_all | solution.py:256
  212.9 13.0 %all-to-all-done.6 = f32[8,136,64]{1,2,0:T(8,128)} async-done(((f32[8,136,64]{1,2,0:T(8,128)}), f32[8,136,64]{1,2,0:T(8,128)}, u32[]{:S(2)}, u32[]{:S(2)}) %all-to-all-start.6) | async-done | bytes 278560 | tf_op jit(solution)/shard_map/all_to_all | solution.py:256
  225.9 1.0 slice_reduce_fusion
  228.4 5.6 %add_bitcast_fusion = f32[4,16,32,128]{3,2,1,0:T(8,128)} fusion(f32[2,4,16,32,128]{4,3,2,1,0:T(8,128)} %copy-done.4, f32[2,4,16,32,128]{4,3,2,1,0:T(8,128)S(1)} %copy-done.3, f32[]{:T(128)} %bitcast.95, f32[]{:T(128)} %bitcast.94, f32[]{:T(128)} %bitcast.93, f32[]{:T(128)} %bitcast.92), kind=kLoop, calls=%fused_computation.90 | loop fusion | flops 1835008 | bytes 5242896 | tf_op jit(solution)/shard_map/add | solution.py:374
  234.1 3.7 %all-to-all-start.7 = ((f32[4,16,32,128]{3,2,1,0:T(8,128)}), f32[4,16,32,128]{3,2,1,0:T(8,128)S(1)}, u32[]{:S(2)}, u32[]{:S(2)}) async-start(f32[4,16,32,128]{3,2,1,0:T(8,128)} %add_bitcast_fusion), calls=%async_computation.7 | async-start | bytes 2097152 | tf_op jit(solution)/shard_map/all_to_all | solution.py:376
  237.8 1.0 slice.340
  241.1 0.8 add_reduce_fusion
  242.7 8.5 %all-to-all-done.7 = f32[4,16,32,128]{3,2,1,0:T(8,128)S(1)} async-done(((f32[4,16,32,128]{3,2,1,0:T(8,128)}), f32[4,16,32,128]{3,2,1,0:T(8,128)S(1)}, u32[]{:S(2)}, u32[]{:S(2)}) %all-to-all-start.7) | async-done | bytes 1048608 | tf_op jit(solution)/shard_map/all_to_all | solution.py:376
  (256 shorter events, 37.3 us)
Async XLA Ops:
  0.6 2.1 copy-start.36
  3.7 1.2 copy-start.11
  5.8 17.0 %copy-start.5 = (f32[16,128,128]{2,1,0:T(8,128)S(1)}, f32[16,128,128]{2,1,0:T(8,128)}, u32[]{:S(2)}) copy-start(f32[16,128,128]{2,1,0:T(8,128)} %pot_ref.3) | copy-start | bytes 3145732
  5.8 17.0 %copy-start.6 = (s32[1024]{0:T(1024)S(1)}, s32[1024]{0:T(1024)}, u32[]{:S(2)}) copy-start(s32[1024]{0:T(1024)} %pos_ref.5) | copy-start | bytes 12292
  6.6 16.3 %copy-start = (bf16[4,2,256,256]{3,2,1,0:T(8,128)(2,1)S(1)}, bf16[4,2,256,256]{3,2,1,0:T(8,128)(2,1)}, u32[]{:S(2)}) copy-start(bf16[4,2,256,256]{3,2,1,0:T(8,128)(2,1)} %constant.57.clone.table_ref) | copy-start | bytes 3145732
  56.9 1.2 copy-start.12
  56.9 1.5 copy-start.16
  58.5 5.9 %copy-start.41 = (f32[2048]{0:T(1024)S(1)}, f32[2048]{0:T(1024)}, u32[]{:S(2)}) copy-start(f32[2048]{0:T(1024)} %param.16) | copy-start | bytes 24580
  58.5 5.9 %copy-start.51 = (f32[2]{0:T(128)S(1)}, f32[2]{0:T(128)}, u32[]{:S(2)}) copy-start(f32[2]{0:T(128)} %param.15) | copy-start | bytes 28
  58.5 16.4 %copy-start.7 = (f32[2,64,2048]{2,1,0:T(8,128)S(1)}, f32[2,64,2048]{2,1,0:T(8,128)}, u32[]{:S(2)}) copy-start(f32[2,64,2048]{2,1,0:T(8,128)} %param.19) | copy-start | bytes 3145732
  60.9 9.0 %all-to-all-start.2 = ((f32[8,8,128]{2,1,0:T(8,128)}), f32[8,8,128]{2,1,0:T(8,128)S(1)}, u32[]{:S(2)}, u32[]{:S(2)}) async-start(f32[8,8,128]{2,1,0:T(8,128)} %broadcast_in_dim.35), calls=%async_computation.2 | async-start | bytes 65536 | tf_op jit(solution)/shard_map/all_to_all | solution.py:266
  64.5 14.8 %copy-start.24 = (f32[2,2048]{1,0:T(2,128)}, f32[2,2048]{1,0:T(2,128)S(1)}, u32[]{:S(2)}) copy-start(f32[2,2048]{1,0:T(2,128)S(1)} %get-tuple-element.61) | copy-start | bytes 49156
  64.5 14.8 %copy-start.29 = (f32[2,2048]{1,0:T(2,128)}, f32[2,2048]{1,0:T(2,128)S(1)}, u32[]{:S(2)}) copy-start(f32[2,2048]{1,0:T(2,128)S(1)} %get-tuple-element.62) | copy-start | bytes 49156
  70.8 4.8 %copy-start.17 = (f32[128,2048]{1,0:T(8,128)S(1)}, f32[128,2048]{1,0:T(8,128)}, u32[]{:S(2)}) copy-start(f32[128,2048]{1,0:T(8,128)} %copy-done.15) | copy-start | bytes 3145732
  74.6 4.7 %copy-start.21 = (f32[2,2,2048]{2,1,0:T(2,128)}, f32[2,2,2048]{2,1,0:T(2,128)S(1)}, u32[]{:S(2)}) copy-start(f32[2,2,2048]{2,1,0:T(2,128)S(1)} %get-tuple-element.38) | copy-start | bytes 98308
  77.7 6.4 %copy-start.52 = (s32[16]{0:T(128)S(1)}, s32[16]{0:T(128)}, u32[]{:S(2)}) copy-start(s32[16]{0:T(128)} %param.22) | copy-start | bytes 196
  79.8 22.6 %copy-start.1 = (f32[16,128,128]{2,1,0:T(8,128)S(1)}, f32[16,128,128]{2,1,0:T(8,128)}, u32[]{:S(2)}) copy-start(f32[16,128,128]{2,1,0:T(8,128)} %pot_ref.5) | copy-start | bytes 3145732
  80.6 18.8 %all-to-all-start.3 = ((f32[8,136,64]{1,2,0:T(8,128)}), f32[8,136,64]{1,2,0:T(8,128)S(1)}, u32[]{:S(2)}, u32[]{:S(2)}) async-start(f32[8,136,64]{1,2,0:T(8,128)} %pad_maximum_fusion.3), calls=%async_computation.3 | async-start | bytes 1048576 | tf_op jit(solution)/shard_map/all_to_all | solution.py:256
  123.1 1.4 copy-start.2
  127.2 7.9 %copy-start.40 = (f32[2,2048]{1,0:T(2,128)S(1)}, f32[2,2048]{1,0:T(2,128)}, u32[]{:S(2)}) copy-start(f32[2,2048]{1,0:T(2,128)} %fusion.146) | copy-start | bytes 49156
  127.2 9.5 %copy-start.39 = (f32[2,2048]{1,0:T(2,128)S(1)}, f32[2,2048]{1,0:T(2,128)}, u32[]{:S(2)}) copy-start(f32[2,2048]{1,0:T(2,128)} %fusion.128) | copy-start | bytes 49156
  127.2 18.9 %all-to-all-start.4 = ((f32[8,136,64]{1,2,0:T(8,128)}), f32[8,136,64]{1,2,0:T(8,128)S(1)}, u32[]{:S(2)}, u32[]{:S(2)}) async-start(f32[8,136,64]{1,2,0:T(8,128)} %pad_maximum_fusion.4), calls=%async_computation.4 | async-start | bytes 1048576 | tf_op jit(solution)/shard_map/all_to_all | solution.py:256
  131.4 15.0 %copy-start.47 = (f32[2,64,2]{1,2,0:T(2,128)}, f32[2,64,2]{1,2,0:T(2,128)S(1)}, u32[]{:S(2)}) copy-start(f32[2,64,2]{1,2,0:T(2,128)S(1)} %copy.184) | copy-start | bytes 3076
  131.4 7.6 %copy-start.8 = (f32[2,64,2048]{2,1,0:T(8,128)S(1)}, f32[2,64,2048]{2,1,0:T(8,128)}, u32[]{:S(2)}) copy-start(f32[2,64,2048]{2,1,0:T(8,128)} %param.19) | copy-start | bytes 3145732
  147.2 1.2 copy-start.13
  147.2 1.5 copy-start.18
  148.7 1.3 copy-start.9
  149.6 1.8 copy-start.43
  149.7 27.4 %copy-start.27 = (f32[2,2,2048]{2,1,0:T(2,128)}, f32[2,2,2048]{2,1,0:T(2,128)S(1)}, u32[]{:S(2)}) copy-start(f32[2,2,2048]{2,1,0:T(2,128)S(1)} %get-tuple-element.36) | copy-start | bytes 98308
  157.9 18.8 %all-to-all-start.5 = ((f32[8,136,64]{1,2,0:T(8,128)}), f32[8,136,64]{1,2,0:T(8,128)S(1)}, u32[]{:S(2)}, u32[]{:S(2)}) async-start(f32[8,136,64]{1,2,0:T(8,128)} %pad_maximum_fusion.5), calls=%async_computation.5 | async-start | bytes 1048576 | tf_op jit(solution)/shard_map/all_to_all | solution.py:256
  177.1 3.8 %copy-start.45 = (f32[2]{0:T(128)}, f32[2]{0:T(128)S(1)}, u32[]{:S(2)}) copy-start(f32[2]{0:T(128)S(1)} %slice_divide_fusion) | copy-start | bytes 28
  182.8 22.2 %copy-start.50 = (f32[2]{0:T(128)S(1)}, f32[2]{0:T(128)}, u32[]{:S(2)}) copy-start(f32[2]{0:T(128)} %get-tuple-element.31) | copy-start | bytes 28
  203.5 1.3 copy-start.4
  204.8 6.2 %copy-start.46 = (f32[2]{0:T(128)S(1)}, f32[2]{0:T(128)}, u32[]{:S(2)}) copy-start(f32[2]{0:T(128)} %copy-done.45) | copy-start | bytes 28
  204.8 6.2 %copy-start.48 = (f32[2,64,2]{1,2,0:T(2,128)S(1)}, f32[2,64,2]{1,2,0:T(2,128)}, u32[]{:S(2)}) copy-start(f32[2,64,2]{1,2,0:T(2,128)} %copy-done.47) | copy-start | bytes 3076
  204.8 6.2 %copy-start.53 = (f32[64]{0:T(128)S(1)}, f32[64]{0:T(128)}, u32[]{:S(2)}) copy-start(f32[64]{0:T(128)} %param.21) | copy-start | bytes 772
  204.8 6.2 %copy-start.54 = (f32[64]{0:T(128)S(1)}, f32[64]{0:T(128)}, u32[]{:S(2)}) copy-start(f32[64]{0:T(128)} %param.20) | copy-start | bytes 772
  204.8 6.2 %copy-start.55 = (s32[64]{0:T(128)S(1)}, s32[64]{0:T(128)}, u32[]{:S(2)}) copy-start(s32[64]{0:T(128)} %convert_reduce_fusion) | copy-start | bytes 772
  204.8 6.5 %copy-start.10 = (f32[2,64,2048]{2,1,0:T(8,128)S(1)}, f32[2,64,2048]{2,1,0:T(8,128)}, u32[]{:S(2)}) copy-start(f32[2,64,2048]{2,1,0:T(8,128)} %param.19) | copy-start | bytes 3145732
  205.2 6.7 %copy-start.35 = (f32[2,8,2]{2,1,0:T(8,128)S(1)}, f32[2,8,2]{2,1,0:T(8,128)}, u32[]{:S(2)}) copy-start(f32[2,8,2]{2,1,0:T(8,128)} %copy-done.34) | copy-start | bytes 388
  205.2 6.7 %copy-start.38 = (f32[2,2048]{1,0:T(2,128)S(1)}, f32[2,2048]{1,0:T(2,128)}, u32[]{:S(2)}) copy-start(f32[2,2048]{1,0:T(2,128)} %fusion.139) | copy-start | bytes 49156
  205.4 6.8 %copy-start.37 = (f32[2,2048]{1,0:T(2,128)S(1)}, f32[2,2048]{1,0:T(2,128)}, u32[]{:S(2)}) copy-start(f32[2,2048]{1,0:T(2,128)} %fusion.123) | copy-start | bytes 49156
  206.2 20.8 %copy-start.49 = (f32[2]{0:T(128)S(1)}, f32[2]{0:T(128)}, u32[]{:S(2)}) copy-start(f32[2]{0:T(128)} %get-tuple-element.33) | copy-start | bytes 28
  206.2 22.2 %copy-start.3 = (f32[2,4,16,32,128]{4,3,2,1,0:T(8,128)S(1)}, f32[2,4,16,32,128]{4,3,2,1,0:T(8,128)}, u32[]{:S(2)}) copy-start(f32[2,4,16,32,128]{4,3,2,1,0:T(8,128)} %copy-done.2) | copy-start | bytes 6291460
  206.2 19.7 %all-to-all-start.6 = ((f32[8,136,64]{1,2,0:T(8,128)}), f32[8,136,64]{1,2,0:T(8,128)}, u32[]{:S(2)}, u32[]{:S(2)}) async-start(f32[8,136,64]{1,2,0:T(8,128)} %pad_maximum_fusion.6), calls=%async_computation.6 | async-start | bytes 1048576 | tf_op jit(solution)/shard_map/all_to_all | solution.py:256
  234.1 17.2 %all-to-all-start.7 = ((f32[4,16,32,128]{3,2,1,0:T(8,128)}), f32[4,16,32,128]{3,2,1,0:T(8,128)S(1)}, u32[]{:S(2)}, u32[]{:S(2)}) async-start(f32[4,16,32,128]{3,2,1,0:T(8,128)} %add_bitcast_fusion), calls=%async_computation.7 | async-start | bytes 2097152 | tf_op jit(solution)/shard_map/all_to_all | solution.py:376
  239.6 1.2 copy-start.14
  239.6 1.5 copy-start.19
  (14 other events, 12.1 us)
